TPU v7x, 32 devices: a whole 2x2x4 slice. The times are simulated.
32 devices in a mesh: gx: 4 (over y, x), gy: 2 (over core), gz: 4 (over z).
Axes of the slice: x: 2, y: 2, z: 4, core: 2. Of those that a mesh axis runs over, the one named last changes fastest.
Arguments:
- leaf_multipoles: float32 [32768, 152], P(('gx', 'gy', 'gz')), may hold values from -6 to 6
- upward_ops: float32 [8, 152, 152], replicated, may hold values from -0.15625 to 0.15625
- transfer_ops: float32 [16, 152, 152], replicated, may hold values from -0.15625 to 0.15625
- downward_ops: float32 [8, 152, 152], replicated, may hold values from -0.5 to 0.5
- send_cells: int32 [32, 4, 32], P(('gx', 'gy', 'gz')), may hold values from 0 to 127
- send_count: int32 [32, 4], P(('gx', 'gy', 'gz')), may hold values from 1 to 32, as said below
- list_source: int32 [32, 16, 128], P(('gx', 'gy', 'gz')), may hold values from 0 to 255
- list_target: int32 [32, 16, 128], P(('gx', 'gy', 'gz')), may hold values from 0 to 127, as said below
- list_count: int32 [32, 16], P(('gx', 'gy', 'gz')), may hold values from 32 to 128, as said below
Outputs:
- leaf_locals: float32 [32768, 152], P(('gx', 'gy', 'gz'))
Inputs may be any that keep to these rules, and one draw needn't show every extreme that they name: `send_count`: in each row one count equals 32, at a peer drawn from the seed. `list_count`: in each row one count equals 128, at an operator drawn from the seed. `list_target`: for each device and operator the 128 entries are a permutation of the local cells, so the used slots name distinct targets.
All inputs are finite; a program needn't handle non-finite values.
Results may differ from a plain program's by a relative error of at most 0.0003.
Values sent between devices are 32-bit elements; how exact they have to be, the bound alone decides.
A program may use at most 64 MiB of HBM per device.

v0:
```python
import jax
import jax.numpy as jnp
from jax import lax
from jax.sharding import PartitionSpec as P


def local(
    leaf_multipoles,
    upward_ops,
    transfer_ops,
    downward_ops,
    send_cells,
    send_count,
    list_source,
    list_target,
    list_count,
):
    highest = lax.Precision.HIGHEST
    coef_count = leaf_multipoles.shape[1]
    cell_count = leaf_multipoles.shape[0] // 8
    op_count = transfer_ops.shape[0]
    slot_count = send_cells.shape[2]
    peer_count = send_cells.shape[1]
    list_width = list_source.shape[2]
    cell_multipoles = jnp.einsum(
        "ckp,kpq->cq",
        leaf_multipoles.reshape(cell_count, 8, coef_count),
        upward_ops,
        precision=highest,
    )
    octant_sums = cell_multipoles.reshape(cell_count // 8, 8, coef_count).sum(0)
    coarse = (8.0 / cell_count) ** 0.5 * jnp.einsum(
        "kp,kpq->q", octant_sums, upward_ops, precision=highest
    )
    device_total = lax.axis_size(("gx", "gy", "gz"))
    group_size = lax.axis_size("gz")
    myself = lax.axis_index(("gx", "gy", "gz"))
    factor = (32.0 / device_total) ** 0.5
    op_ids = jnp.arange(op_count, dtype=jnp.int32)
    every_top = lax.all_gather(coarse[None], ("gx", "gy", "gz"), axis=0, tiled=True)
    others = jnp.arange(device_total, dtype=jnp.int32)
    mixed_ids = jnp.bitwise_xor(others, myself)
    onehot = (
        (mixed_ids[None] % op_count == op_ids[:, None]) & (mixed_ids[None] >= group_size)
    ).astype(jnp.float32)
    grouped_top = jnp.dot(onehot, every_top, precision=highest)
    coarse_local = factor * jnp.einsum("kp,kpq->q", grouped_top, transfer_ops, precision=highest)
    slot_ids = jnp.arange(slot_count, dtype=jnp.int32)
    active_slots = (slot_ids[None] < send_count[0][:, None]).astype(jnp.float32)
    outgoing = cell_multipoles[send_cells[0]] * active_slots[..., None]
    incoming = lax.all_to_all(outgoing, "gz", split_axis=0, concat_axis=0, tiled=True)
    table = jnp.concatenate(
        [cell_multipoles, incoming.reshape(peer_count * slot_count, coef_count)], 0
    )
    active = (jnp.arange(list_width, dtype=jnp.int32)[None] < list_count[0][:, None]).astype(
        jnp.float32
    )
    initial = jnp.zeros((cell_count, coef_count), jnp.float32)

    def one_operator(total, entry):
        source, target, weights, operator = entry
        product = jnp.dot(table[source], operator, precision=highest) * weights[:, None]
        return (total.at[target].add(product), None)

    total, unused = lax.scan(
        one_operator, initial, (list_source[0], list_target[0], active, transfer_ops)
    )
    downward_top = jnp.einsum("p,kpq->kq", coarse_local, downward_ops, precision=highest)
    cell_locals = (total.reshape(cell_count // 8, 8, coef_count) + downward_top[None]).reshape(
        cell_count, coef_count
    )
    return jnp.einsum("cp,kpq->ckq", cell_locals, downward_ops, precision=highest).reshape(
        8 * cell_count, coef_count
    )


def solution(mesh):
    return jax.shard_map(
        local,
        mesh=mesh,
        in_specs=(
            P(("gx", "gy", "gz"), None),
            P(),
            P(),
            P(),
            P(("gx", "gy", "gz"), None, None),
            P(("gx", "gy", "gz"), None),
            P(("gx", "gy", "gz"), None, None),
            P(("gx", "gy", "gz"), None, None),
            P(("gx", "gy", "gz"), None),
        ),
        out_specs=P(("gx", "gy", "gz"), None),
        check_vma=False,
    )
```

profile of v0, /device:TPU:0, one launch (start us, length us, event | category | flops | bytes accessed | tf_op | source)
XLA Modules:
  0.0 134.8 jit_solution(17625437415893828453)
XLA Ops:
  0.0 0.8 compare_select_fusion.2
  0.9 0.7 fusion.19
  1.6 1.4 %copy.18 = f32[1024,152]{1,0:T(8,128)S(1)} copy(f32[1024,152]{0,1:T(8,128)} %param.11) | data formatting | bytes 1245184 | tf_op args[0]
  3.0 2.9 %convolution_bitcast_fusion = f32[128,152]{0,1:T(8,128)S(1)} fusion(f32[8,152,152]{2,1,0:T(8,128)S(1)} %copy-done, f32[128,8,152]{2,1,0:T(8,128)S(1)} %bitcast.75), kind=kOutput, calls=%fused_computation.18 | convolution fusion | flops 283901952 | bytes 1439744 | tf_op jit(solution)/shard_map/ckp,kpq->cq/dot_general | solution.py:25
  6.0 0.8 gather_fusion.1
  6.8 0.7 broadcast_multiply_fusion
  7.5 6.3 %all-to-all-start = ((f32[4,32,152]{2,1,0:T(8,128)}), f32[4,32,152]{2,1,0:T(8,128)S(1)}, u32[]{:S(2)}, u32[]{:S(2)}) async-start(f32[4,32,152]{2,1,0:T(8,128)} %broadcast_multiply_fusion), calls=%async_computation | async-start | bytes 262144 | tf_op jit(solution)/shard_map/all_to_all | solution.py:51
  14.6 41.0 %all-reduce = f32[4864]{0:T(1024)S(1)} all-reduce(f32[4864]{0:T(1024)S(1)} %multiply_dynamic-update-slice_fusion), channel_id=2, replica_groups=mesh['gx'=4,'gy'=2,'gz'=4] {'gx','gy','gz'}, use_global_device_ids=true, to_apply=%add | all-reduce | flops 4864 | bytes 38912
  55.7 1.6 %copy.26 = f32[8,152,152]{1,2,0:T(8,128)} copy(f32[8,152,152]{2,1,0:T(8,128)S(1)} %copy-done.1) | data formatting | bytes 1478656 | tf_op args[3]
  57.5 2.9 %convolution_bitcast_fusion.2 = f32[152,1,1]{0,1,2:T(1,128)S(1)} fusion(f32[16,152,152]{2,1,0:T(8,128)} %param.13, f32[16,152,1]{1,0,2:T(8,128)S(1)} %convolution_bitcast_fusion.1), kind=kOutput, calls=%fused_computation.20 | convolution fusion | flops 4435968 | bytes 1488992 | tf_op jit(solution)/shard_map/kp,kpq->q/dot_general | solution.py:47
  60.4 0.7 fusion.22
  61.5 70.6 %while.10 = (s32[]{:T(128)}, f32[128,152]{1,0:T(8,128)S(1)}, s32[16,128]{1,0:T(8,128)}, s32[16,128]{1,0:T(8,128)}, f32[256,152]{1,0:T(8,128)S(1)}, /*index=5*/f3...) while((s32[]{:T(128)}, f32[128,152]{1,0:T(8,128)S(1)}, s32[16,128]{1,0:T(8,128)}, s32[16,128]{1,0:T(8,128)}, ...), condition=%wide.region_2.3_spmd, body=%wide.region_0.2_spmd.sunk | while | flops 35528448 | bytes 865385 | solution.py:65
  61.5 0.8 fusion.37
  62.3 0.8 gather_fusion
  63.1 1.4 %convolution_multiply_fusion.2 = f32[128,152]{0,1:T(8,128)S(1)} fusion(f32[128,152]{1,0:T(8,128)S(1)} %gather_fusion, f32[16,152,152]{2,1,0:T(8,128)} %get-tuple-element.141, s32[]{:T(128)S(6)} %copy.47, f32[128]{0:T(128)S(1)} %fusion.38), kind=kOutput, calls=%fused_computation.3.clone.1 | convolution fusion | flops 35507200 | bytes 311812 | tf_op jit(solution)/shard_map/while/body/eval_jaxpr/dot_general | solution.py:62
  64.6 1.4 %scatter_fusion = f32[128,152]{1,0:T(8,128)S(1)} fusion(f32[128,152]{1,0:T(8,128)S(1)} %get-tuple-element.129, s32[128]{0:T(128)S(1)} %get-tuple-element.118, f32[128,152]{1,0:T(8,128)S(1)} %copy.43), kind=kCustom, calls=%fused_computation.2.clone.1 | custom fusion | flops 19456 | bytes 233984 | tf_op jit(solution)/shard_map/while/body/eval_jaxpr/scatter-add | solution.py:63
  66.7 0.8 gather_fusion
  67.5 1.4 %convolution_multiply_fusion.2 = f32[128,152]{0,1:T(8,128)S(1)} fusion(f32[128,152]{1,0:T(8,128)S(1)} %gather_fusion, f32[16,152,152]{2,1,0:T(8,128)} %get-tuple-element.141, s32[]{:T(128)S(6)} %copy.47, f32[128]{0:T(128)S(1)} %fusion.38), kind=kOutput, calls=%fused_computation.3.clone.1 | convolution fusion | flops 35507200 | bytes 311812 | tf_op jit(solution)/shard_map/while/body/eval_jaxpr/dot_general | solution.py:62
  69.0 1.4 %scatter_fusion = f32[128,152]{1,0:T(8,128)S(1)} fusion(f32[128,152]{1,0:T(8,128)S(1)} %get-tuple-element.129, s32[128]{0:T(128)S(1)} %get-tuple-element.118, f32[128,152]{1,0:T(8,128)S(1)} %copy.43), kind=kCustom, calls=%fused_computation.2.clone.1 | custom fusion | flops 19456 | bytes 233984 | tf_op jit(solution)/shard_map/while/body/eval_jaxpr/scatter-add | solution.py:63
  71.1 0.8 gather_fusion
  71.9 1.4 %convolution_multiply_fusion.2 = f32[128,152]{0,1:T(8,128)S(1)} fusion(f32[128,152]{1,0:T(8,128)S(1)} %gather_fusion, f32[16,152,152]{2,1,0:T(8,128)} %get-tuple-element.141, s32[]{:T(128)S(6)} %copy.47, f32[128]{0:T(128)S(1)} %fusion.38), kind=kOutput, calls=%fused_computation.3.clone.1 | convolution fusion | flops 35507200 | bytes 311812 | tf_op jit(solution)/shard_map/while/body/eval_jaxpr/dot_general | solution.py:62
  73.4 1.4 %scatter_fusion = f32[128,152]{1,0:T(8,128)S(1)} fusion(f32[128,152]{1,0:T(8,128)S(1)} %get-tuple-element.129, s32[128]{0:T(128)S(1)} %get-tuple-element.118, f32[128,152]{1,0:T(8,128)S(1)} %copy.43), kind=kCustom, calls=%fused_computation.2.clone.1 | custom fusion | flops 19456 | bytes 233984 | tf_op jit(solution)/shard_map/while/body/eval_jaxpr/scatter-add | solution.py:63
  75.5 0.8 gather_fusion
  76.3 1.4 %convolution_multiply_fusion.2 = f32[128,152]{0,1:T(8,128)S(1)} fusion(f32[128,152]{1,0:T(8,128)S(1)} %gather_fusion, f32[16,152,152]{2,1,0:T(8,128)} %get-tuple-element.141, s32[]{:T(128)S(6)} %copy.47, f32[128]{0:T(128)S(1)} %fusion.38), kind=kOutput, calls=%fused_computation.3.clone.1 | convolution fusion | flops 35507200 | bytes 311812 | tf_op jit(solution)/shard_map/while/body/eval_jaxpr/dot_general | solution.py:62
  77.8 1.4 %scatter_fusion = f32[128,152]{1,0:T(8,128)S(1)} fusion(f32[128,152]{1,0:T(8,128)S(1)} %get-tuple-element.129, s32[128]{0:T(128)S(1)} %get-tuple-element.118, f32[128,152]{1,0:T(8,128)S(1)} %copy.43), kind=kCustom, calls=%fused_computation.2.clone.1 | custom fusion | flops 19456 | bytes 233984 | tf_op jit(solution)/shard_map/while/body/eval_jaxpr/scatter-add | solution.py:63
  79.9 0.8 gather_fusion
  80.7 1.4 %convolution_multiply_fusion.2 = f32[128,152]{0,1:T(8,128)S(1)} fusion(f32[128,152]{1,0:T(8,128)S(1)} %gather_fusion, f32[16,152,152]{2,1,0:T(8,128)} %get-tuple-element.141, s32[]{:T(128)S(6)} %copy.47, f32[128]{0:T(128)S(1)} %fusion.38), kind=kOutput, calls=%fused_computation.3.clone.1 | convolution fusion | flops 35507200 | bytes 311812 | tf_op jit(solution)/shard_map/while/body/eval_jaxpr/dot_general | solution.py:62
  82.2 1.4 %scatter_fusion = f32[128,152]{1,0:T(8,128)S(1)} fusion(f32[128,152]{1,0:T(8,128)S(1)} %get-tuple-element.129, s32[128]{0:T(128)S(1)} %get-tuple-element.118, f32[128,152]{1,0:T(8,128)S(1)} %copy.43), kind=kCustom, calls=%fused_computation.2.clone.1 | custom fusion | flops 19456 | bytes 233984 | tf_op jit(solution)/shard_map/while/body/eval_jaxpr/scatter-add | solution.py:63
  83.6 0.7 fusion.37
  84.3 0.8 gather_fusion
  85.1 1.4 %convolution_multiply_fusion.2 = f32[128,152]{0,1:T(8,128)S(1)} fusion(f32[128,152]{1,0:T(8,128)S(1)} %gather_fusion, f32[16,152,152]{2,1,0:T(8,128)} %get-tuple-element.141, s32[]{:T(128)S(6)} %copy.47, f32[128]{0:T(128)S(1)} %fusion.38), kind=kOutput, calls=%fused_computation.3.clone.1 | convolution fusion | flops 35507200 | bytes 311812 | tf_op jit(solution)/shard_map/while/body/eval_jaxpr/dot_general | solution.py:62
  86.6 1.4 %scatter_fusion = f32[128,152]{1,0:T(8,128)S(1)} fusion(f32[128,152]{1,0:T(8,128)S(1)} %get-tuple-element.129, s32[128]{0:T(128)S(1)} %get-tuple-element.118, f32[128,152]{1,0:T(8,128)S(1)} %copy.43), kind=kCustom, calls=%fused_computation.2.clone.1 | custom fusion | flops 19456 | bytes 233984 | tf_op jit(solution)/shard_map/while/body/eval_jaxpr/scatter-add | solution.py:63
  88.7 0.8 gather_fusion
  89.5 1.4 %convolution_multiply_fusion.2 = f32[128,152]{0,1:T(8,128)S(1)} fusion(f32[128,152]{1,0:T(8,128)S(1)} %gather_fusion, f32[16,152,152]{2,1,0:T(8,128)} %get-tuple-element.141, s32[]{:T(128)S(6)} %copy.47, f32[128]{0:T(128)S(1)} %fusion.38), kind=kOutput, calls=%fused_computation.3.clone.1 | convolution fusion | flops 35507200 | bytes 311812 | tf_op jit(solution)/shard_map/while/body/eval_jaxpr/dot_general | solution.py:62
  91.0 1.4 %scatter_fusion = f32[128,152]{1,0:T(8,128)S(1)} fusion(f32[128,152]{1,0:T(8,128)S(1)} %get-tuple-element.129, s32[128]{0:T(128)S(1)} %get-tuple-element.118, f32[128,152]{1,0:T(8,128)S(1)} %copy.43), kind=kCustom, calls=%fused_computation.2.clone.1 | custom fusion | flops 19456 | bytes 233984 | tf_op jit(solution)/shard_map/while/body/eval_jaxpr/scatter-add | solution.py:63
  93.2 0.8 gather_fusion
  93.9 1.4 %convolution_multiply_fusion.2 = f32[128,152]{0,1:T(8,128)S(1)} fusion(f32[128,152]{1,0:T(8,128)S(1)} %gather_fusion, f32[16,152,152]{2,1,0:T(8,128)} %get-tuple-element.141, s32[]{:T(128)S(6)} %copy.47, f32[128]{0:T(128)S(1)} %fusion.38), kind=kOutput, calls=%fused_computation.3.clone.1 | convolution fusion | flops 35507200 | bytes 311812 | tf_op jit(solution)/shard_map/while/body/eval_jaxpr/dot_general | solution.py:62
  95.4 1.4 %scatter_fusion = f32[128,152]{1,0:T(8,128)S(1)} fusion(f32[128,152]{1,0:T(8,128)S(1)} %get-tuple-element.129, s32[128]{0:T(128)S(1)} %get-tuple-element.118, f32[128,152]{1,0:T(8,128)S(1)} %copy.43), kind=kCustom, calls=%fused_computation.2.clone.1 | custom fusion | flops 19456 | bytes 233984 | tf_op jit(solution)/shard_map/while/body/eval_jaxpr/scatter-add | solution.py:63
  97.6 0.8 gather_fusion
  98.3 1.4 %convolution_multiply_fusion.2 = f32[128,152]{0,1:T(8,128)S(1)} fusion(f32[128,152]{1,0:T(8,128)S(1)} %gather_fusion, f32[16,152,152]{2,1,0:T(8,128)} %get-tuple-element.141, s32[]{:T(128)S(6)} %copy.47, f32[128]{0:T(128)S(1)} %fusion.38), kind=kOutput, calls=%fused_computation.3.clone.1 | convolution fusion | flops 35507200 | bytes 311812 | tf_op jit(solution)/shard_map/while/body/eval_jaxpr/dot_general | solution.py:62
  99.8 1.4 %scatter_fusion = f32[128,152]{1,0:T(8,128)S(1)} fusion(f32[128,152]{1,0:T(8,128)S(1)} %get-tuple-element.129, s32[128]{0:T(128)S(1)} %get-tuple-element.118, f32[128,152]{1,0:T(8,128)S(1)} %copy.43), kind=kCustom, calls=%fused_computation.2.clone.1 | custom fusion | flops 19456 | bytes 233984 | tf_op jit(solution)/shard_map/while/body/eval_jaxpr/scatter-add | solution.py:63
  102.0 0.8 gather_fusion
  102.7 1.4 %convolution_multiply_fusion.2 = f32[128,152]{0,1:T(8,128)S(1)} fusion(f32[128,152]{1,0:T(8,128)S(1)} %gather_fusion, f32[16,152,152]{2,1,0:T(8,128)} %get-tuple-element.141, s32[]{:T(128)S(6)} %copy.47, f32[128]{0:T(128)S(1)} %fusion.38), kind=kOutput, calls=%fused_computation.3.clone.1 | convolution fusion | flops 35507200 | bytes 311812 | tf_op jit(solution)/shard_map/while/body/eval_jaxpr/dot_general | solution.py:62
  104.3 1.4 %scatter_fusion = f32[128,152]{1,0:T(8,128)S(1)} fusion(f32[128,152]{1,0:T(8,128)S(1)} %get-tuple-element.129, s32[128]{0:T(128)S(1)} %get-tuple-element.118, f32[128,152]{1,0:T(8,128)S(1)} %copy.43), kind=kCustom, calls=%fused_computation.2.clone.1 | custom fusion | flops 19456 | bytes 233984 | tf_op jit(solution)/shard_map/while/body/eval_jaxpr/scatter-add | solution.py:63
  106.4 0.8 gather_fusion
  107.1 1.4 %convolution_multiply_fusion.2 = f32[128,152]{0,1:T(8,128)S(1)} fusion(f32[128,152]{1,0:T(8,128)S(1)} %gather_fusion, f32[16,152,152]{2,1,0:T(8,128)} %get-tuple-element.141, s32[]{:T(128)S(6)} %copy.47, f32[128]{0:T(128)S(1)} %fusion.38), kind=kOutput, calls=%fused_computation.3.clone.1 | convolution fusion | flops 35507200 | bytes 311812 | tf_op jit(solution)/shard_map/while/body/eval_jaxpr/dot_general | solution.py:62
  108.7 1.4 %scatter_fusion = f32[128,152]{1,0:T(8,128)S(1)} fusion(f32[128,152]{1,0:T(8,128)S(1)} %get-tuple-element.129, s32[128]{0:T(128)S(1)} %get-tuple-element.118, f32[128,152]{1,0:T(8,128)S(1)} %copy.43), kind=kCustom, calls=%fused_computation.2.clone.1 | custom fusion | flops 19456 | bytes 233984 | tf_op jit(solution)/shard_map/while/body/eval_jaxpr/scatter-add | solution.py:63
  110.8 0.8 gather_fusion
  111.5 1.4 %convolution_multiply_fusion.2 = f32[128,152]{0,1:T(8,128)S(1)} fusion(f32[128,152]{1,0:T(8,128)S(1)} %gather_fusion, f32[16,152,152]{2,1,0:T(8,128)} %get-tuple-element.141, s32[]{:T(128)S(6)} %copy.47, f32[128]{0:T(128)S(1)} %fusion.38), kind=kOutput, calls=%fused_computation.3.clone.1 | convolution fusion | flops 35507200 | bytes 311812 | tf_op jit(solution)/shard_map/while/body/eval_jaxpr/dot_general | solution.py:62
  113.1 1.4 %scatter_fusion = f32[128,152]{1,0:T(8,128)S(1)} fusion(f32[128,152]{1,0:T(8,128)S(1)} %get-tuple-element.129, s32[128]{0:T(128)S(1)} %get-tuple-element.118, f32[128,152]{1,0:T(8,128)S(1)} %copy.43), kind=kCustom, calls=%fused_computation.2.clone.1 | custom fusion | flops 19456 | bytes 233984 | tf_op jit(solution)/shard_map/while/body/eval_jaxpr/scatter-add | solution.py:63
  115.2 0.8 gather_fusion
  115.9 1.4 %convolution_multiply_fusion.2 = f32[128,152]{0,1:T(8,128)S(1)} fusion(f32[128,152]{1,0:T(8,128)S(1)} %gather_fusion, f32[16,152,152]{2,1,0:T(8,128)} %get-tuple-element.141, s32[]{:T(128)S(6)} %copy.47, f32[128]{0:T(128)S(1)} %fusion.38), kind=kOutput, calls=%fused_computation.3.clone.1 | convolution fusion | flops 35507200 | bytes 311812 | tf_op jit(solution)/shard_map/while/body/eval_jaxpr/dot_general | solution.py:62
  117.5 1.4 %scatter_fusion = f32[128,152]{1,0:T(8,128)S(1)} fusion(f32[128,152]{1,0:T(8,128)S(1)} %get-tuple-element.129, s32[128]{0:T(128)S(1)} %get-tuple-element.118, f32[128,152]{1,0:T(8,128)S(1)} %copy.43), kind=kCustom, calls=%fused_computation.2.clone.1 | custom fusion | flops 19456 | bytes 233984 | tf_op jit(solution)/shard_map/while/body/eval_jaxpr/scatter-add | solution.py:63
  119.6 0.8 gather_fusion
  120.4 1.4 %convolution_multiply_fusion.2 = f32[128,152]{0,1:T(8,128)S(1)} fusion(f32[128,152]{1,0:T(8,128)S(1)} %gather_fusion, f32[16,152,152]{2,1,0:T(8,128)} %get-tuple-element.141, s32[]{:T(128)S(6)} %copy.47, f32[128]{0:T(128)S(1)} %fusion.38), kind=kOutput, calls=%fused_computation.3.clone.1 | convolution fusion | flops 35507200 | bytes 311812 | tf_op jit(solution)/shard_map/while/body/eval_jaxpr/dot_general | solution.py:62
  121.9 1.4 %scatter_fusion = f32[128,152]{1,0:T(8,128)S(1)} fusion(f32[128,152]{1,0:T(8,128)S(1)} %get-tuple-element.129, s32[128]{0:T(128)S(1)} %get-tuple-element.118, f32[128,152]{1,0:T(8,128)S(1)} %copy.43), kind=kCustom, calls=%fused_computation.2.clone.1 | custom fusion | flops 19456 | bytes 233984 | tf_op jit(solution)/shard_map/while/body/eval_jaxpr/scatter-add | solution.py:63
  124.0 0.8 gather_fusion
  124.8 1.4 %convolution_multiply_fusion.2 = f32[128,152]{0,1:T(8,128)S(1)} fusion(f32[128,152]{1,0:T(8,128)S(1)} %gather_fusion, f32[16,152,152]{2,1,0:T(8,128)} %get-tuple-element.141, s32[]{:T(128)S(6)} %copy.47, f32[128]{0:T(128)S(1)} %fusion.38), kind=kOutput, calls=%fused_computation.3.clone.1 | convolution fusion | flops 35507200 | bytes 311812 | tf_op jit(solution)/shard_map/while/body/eval_jaxpr/dot_general | solution.py:62
  126.3 1.4 %scatter_fusion = f32[128,152]{1,0:T(8,128)S(1)} fusion(f32[128,152]{1,0:T(8,128)S(1)} %get-tuple-element.129, s32[128]{0:T(128)S(1)} %get-tuple-element.118, f32[128,152]{1,0:T(8,128)S(1)} %copy.43), kind=kCustom, calls=%fused_computation.2.clone.1 | custom fusion | flops 19456 | bytes 233984 | tf_op jit(solution)/shard_map/while/body/eval_jaxpr/scatter-add | solution.py:63
  128.4 0.8 gather_fusion
  129.2 1.4 %convolution_multiply_fusion.2 = f32[128,152]{0,1:T(8,128)S(1)} fusion(f32[128,152]{1,0:T(8,128)S(1)} %gather_fusion, f32[16,152,152]{2,1,0:T(8,128)} %get-tuple-element.141, s32[]{:T(128)S(6)} %copy.47, f32[128]{0:T(128)S(1)} %fusion.38), kind=kOutput, calls=%fused_computation.3.clone.1 | convolution fusion | flops 35507200 | bytes 311812 | tf_op jit(solution)/shard_map/while/body/eval_jaxpr/dot_general | solution.py:62
  130.7 1.4 %scatter_fusion = f32[128,152]{1,0:T(8,128)S(1)} fusion(f32[128,152]{1,0:T(8,128)S(1)} %get-tuple-element.129, s32[128]{0:T(128)S(1)} %get-tuple-element.118, f32[128,152]{1,0:T(8,128)S(1)} %copy.43), kind=kCustom, calls=%fused_computation.2.clone.1 | custom fusion | flops 19456 | bytes 233984 | tf_op jit(solution)/shard_map/while/body/eval_jaxpr/scatter-add | solution.py:63
  132.1 1.1 fusion.9
  133.7 1.1 copy.28
  (89 shorter events, 14.0 us)
Async XLA Ops:
  0.0 3.0 %copy-start = (f32[8,152,152]{2,1,0:T(8,128)S(1)}, f32[8,152,152]{2,1,0:T(8,128)}, u32[]{:S(2)}) copy-start(f32[8,152,152]{2,1,0:T(8,128)} %param.12) | copy-start | bytes 2217988
  6.8 49.0 %copy-start.1 = (f32[8,152,152]{2,1,0:T(8,128)S(1)}, f32[8,152,152]{2,1,0:T(8,128)}, u32[]{:S(2)}) copy-start(f32[8,152,152]{2,1,0:T(8,128)} %param.14) | copy-start | bytes 2217988
  7.5 53.6 %all-to-all-start = ((f32[4,32,152]{2,1,0:T(8,128)}), f32[4,32,152]{2,1,0:T(8,128)S(1)}, u32[]{:S(2)}, u32[]{:S(2)}) async-start(f32[4,32,152]{2,1,0:T(8,128)} %broadcast_multiply_fusion), calls=%async_computation | async-start | bytes 262144 | tf_op jit(solution)/shard_map/all_to_all | solution.py:51
  60.4 0.7 copy-start.3
  61.4 70.6 %copy-start.2 = (f32[8,152,152]{1,2,0:T(8,128)S(1)}, f32[8,152,152]{1,2,0:T(8,128)}, u32[]{:S(2)}) copy-start(f32[8,152,152]{1,2,0:T(8,128)} %copy.26) | copy-start | bytes 2217988
where the time goes:
time: 136 us; the launch traced here: 135 us
  blocking collectives  41 us (30%)
  other arithmetic  35.8 us (26%)
  matrix products  31 us (23%)
  local copies, waits for them, and re-layouts  19.8 us (15%)
  starting transfers between devices  6.32 us (5%)
    unnamed x1, blocking collectives  41 us
    dot_general x16, matrix products, one_operator(): jnp.dot(table[source], operator, precision=highest) * weights[:, None]  22.6 us
    scatter-add x16, other arithmetic, one_operator(): return (total.at[target].add(product), None)  21.7 us
    gather x16, local copies, waits for them, and re-layouts, one_operator(): table[source]  12.1 us
    select_n x16, other arithmetic, one_operator(): return (total.at[target].add(product), None)  11.6 us
    all_to_all x1, starting transfers between devices, local(): lax.all_to_all(outgoing, 'gz', split_axis=0, concat_axis=0, tiled=True)  6.32 us
    unnamed x11, local copies, waits for them, and re-layouts  3.04 us
    dot_general x1, matrix products, local(): jnp.einsum('kp,kpq->q', grouped_top, transfer_ops, precision=highest)  2.88 us
  transfers between devices with their start and end apart: 1, of which 0 were waited for; matrix products, arithmetic and copies ran while one was open for 5% of the time, Pallas kernels for 0%

commit v1 on v0

v1 whole, which is shorter than its diff:
```python
import functools

import jax
import jax.numpy as jnp
from jax import lax
from jax.experimental import pallas as pl
from jax.experimental.pallas import tpu as pltpu
from jax.sharding import PartitionSpec as P

MESH = pl.DeviceIdType.MESH
F32 = jnp.float32
BF16 = jnp.bfloat16
NT = (((1,), (1,)), ((), ()))
TN = (((0,), (0,)), ((), ()))


def split(value):
    high = value.astype(BF16)
    return high, (value - high.astype(F32)).astype(BF16)


def dot(a, b):
    return jnp.dot(a, b, preferred_element_type=F32)


def dot3(a, b):
    return dot(a[0], b[0]) + dot(a[0], b[1]) + dot(a[1], b[0])


def xor(a, b, size):
    total, bit = 0, 1
    while bit < size:
        total = total + ((a // bit + b // bit) % 2) * bit
        bit *= 2
    return total


def equal(row, length):
    rows = lax.broadcasted_iota(jnp.int32, (length, row.shape[1]), 0)
    return jnp.where(rows == row, 1.0, 0.0).astype(BF16)


def kernel(
    sizes,
    leaf_hbm, up_hbm, transfer_hbm, down_hbm,
    cells_hbm, sends_hbm, source_hbm, target_hbm, counts_hbm,
    out_ref,
    leaf, up, transfer, down,
    cells, sends, source, target, counts,
    up_high, up_low, transfer_high, transfer_low, down_high, down_low,
    choose, outgoing, received, top_row, tops, picked_high, picked_low,
    load_sem, send_sem, recv_sem, top_send_sem, top_recv_sem,
):
    n_gx, n_gy, n_gz = sizes
    devices = n_gx * n_gy * n_gz
    cell_count, _, coefs = leaf.shape
    ops = transfer.shape[0]
    slots = cells.shape[1]
    rows = cell_count + n_gz * slots
    i_gx, i_gy, i_gz = lax.axis_index("gx"), lax.axis_index("gy"), lax.axis_index("gz")

    def peer(x):
        return (
            xor(i_gx, x // (n_gz * n_gy), n_gx),
            xor(i_gy, (x // n_gz) % n_gy, n_gy),
            xor(i_gz, x % n_gz, n_gz),
        )

    def each(low, high, body):
        if devices <= 64:
            for x in range(low, high):
                body(x)
        else:
            lax.fori_loop(low, high, lambda x, c: (body(x), c)[1], 0)

    loads = [
        pltpu.make_async_copy(src, dst, load_sem.at[i])
        for i, (src, dst) in enumerate(
            [
                (source_hbm.at[0], source),
                (target_hbm.at[0], target),
                (counts_hbm, counts),
                (cells_hbm.at[0], cells),
                (sends_hbm, sends),
                (leaf_hbm, leaf),
                (up_hbm, up),
                (transfer_hbm, transfer),
                (down_hbm, down),
            ]
        )
    ]
    for load in loads:
        load.start()

    barrier = pltpu.get_barrier_semaphore()
    each(
        1,
        devices,
        lambda x: pl.semaphore_signal(barrier, inc=1, device_id=peer(x), device_id_type=MESH),
    )

    for load in loads[:5]:
        load.wait()
    lane = lax.broadcasted_iota(jnp.int32, (1, target.shape[1]), 1)
    for k in range(ops):
        used = jnp.where(lane < counts[0:1, k : k + 1], target[k : k + 1, :], -1)
        choose[pl.ds(k * cell_count, cell_count), :] = lax.dot_general(
            equal(used, cell_count),
            equal(source[k : k + 1, :], rows),
            NT,
            preferred_element_type=F32,
        ).astype(BF16)
    lane = lax.broadcasted_iota(jnp.int32, (1, slots), 1)
    wanted = jnp.concatenate(
        [
            jnp.where(lane < sends[0:1, s : s + 1], cells[s : s + 1, :], -1)
            for s in range(n_gz)
        ],
        axis=1,
    )
    pick = equal(wanted, cell_count)

    loads[5].wait()
    loads[6].wait()
    cell = jnp.zeros((cell_count, coefs), F32)
    for k in range(8):
        up_high[k], up_low[k] = split(up[k])
        cell = cell + dot3(split(leaf[:, k, :]), (up_high[k], up_low[k]))
    cell_high, cell_low = split(cell)
    out_rows = lax.dot_general(pick, cell_high, TN, preferred_element_type=F32) + lax.dot_general(
        pick, cell_low, TN, preferred_element_type=F32
    )
    outgoing[...] = out_rows.reshape(n_gz, slots, coefs)
    pl.semaphore_wait(barrier, devices - 1)

    def cell_copy(x):
        to = peer(x)
        return pltpu.make_async_remote_copy(
            src_ref=outgoing.at[to[2]],
            dst_ref=received.at[i_gz],
            send_sem=send_sem.at[x],
            recv_sem=recv_sem.at[x],
            device_id=to,
            device_id_type=MESH,
        )

    cell_copies = [cell_copy(x) for x in range(1, n_gz)]
    for copy in cell_copies:
        copy.start()

    octants = split(cell.reshape(cell_count // 8, 8, coefs).sum(0))
    top = jnp.zeros((8, coefs), F32)
    eight = lax.broadcasted_iota(jnp.int32, (8, coefs), 0)
    for k in range(8):
        top = top + jnp.where(eight == k, dot3(octants, (up_high[k], up_low[k])), 0.0)
    top_row[...] = (8.0 / cell_count) ** 0.5 * top.sum(0, keepdims=True)

    def send_top(x):
        pltpu.make_async_remote_copy(
            src_ref=top_row,
            dst_ref=tops.at[x],
            send_sem=top_send_sem,
            recv_sem=top_recv_sem,
            device_id=peer(x),
            device_id_type=MESH,
        ).start()

    each(n_gz, devices, send_top)

    loads[7].wait()
    for k in range(ops):
        transfer_high[k], transfer_low[k] = split(transfer[k])
    loads[8].wait()
    for k in range(8):
        down_high[k], down_low[k] = split(down[k])
    received[i_gz] = outgoing[i_gz]

    for copy in cell_copies:
        copy.wait_recv()
    got_high, got_low = split(received[...].reshape(n_gz * slots, coefs))
    table_high = jnp.concatenate([cell_high, got_high], axis=0)
    table_low = jnp.concatenate([cell_low, got_low], axis=0)
    for k in range(ops):
        chosen = choose[pl.ds(k * cell_count, cell_count), :]
        picked_high[k, 0:cell_count, :] = dot(chosen, table_high).astype(BF16)
        picked_low[k, 0:cell_count, :] = dot(chosen, table_low).astype(BF16)

    far = tops.at[pl.ds(n_gz, devices - n_gz)]
    pltpu.make_async_copy(far, far, top_recv_sem).wait()
    for k in range(ops):
        extra = jnp.zeros((1, coefs), F32)
        for x in range(k, devices, ops):
            if x >= n_gz:
                extra = extra + tops[x]
        picked_high[k, cell_count : cell_count + 16, :], picked_low[
            k, cell_count : cell_count + 16, :
        ] = split(jnp.broadcast_to(extra, (16, coefs)))
    total = jnp.zeros((cell_count + 16, coefs), F32)
    for k in range(ops):
        total = total + dot3(
            (picked_high[k], picked_low[k]), (transfer_high[k], transfer_low[k])
        )
    coarse = split((32.0 / devices) ** 0.5 * total[cell_count:])
    coarse_down = jnp.zeros((8, coefs), F32)
    for k in range(8):
        coarse_down = coarse_down + jnp.where(
            eight == k, dot3(coarse, (down_high[k], down_low[k]))[0:8], 0.0
        )
    near = total[0:cell_count].reshape(cell_count // 8, 8, coefs)
    local_cells = split((near + coarse_down[None]).reshape(cell_count, coefs))
    for k in range(8):
        out_ref[:, k, :] = dot3(local_cells, (down_high[k], down_low[k]))

    for copy in cell_copies:
        copy.wait_send()
    pltpu.make_async_copy(far, far, top_send_sem).wait()


def local(sizes, leaf_multipoles, upward_ops, transfer_ops, downward_ops, *lists):
    leaves, coefs = leaf_multipoles.shape
    cell_count = leaves // 8
    ops = transfer_ops.shape[0]
    send_cells, send_count, list_source, list_target, list_count = lists
    n_gz, slots = send_cells.shape[1:]
    devices = sizes[0] * sizes[1] * sizes[2]
    rows = cell_count + n_gz * slots
    vmem = pltpu.VMEM
    weights = lambda n: [vmem((n, coefs, coefs), BF16)] * 2
    out = pl.pallas_call(
        functools.partial(kernel, sizes),
        out_shape=jax.ShapeDtypeStruct((cell_count, 8, coefs), F32),
        in_specs=[pl.BlockSpec(memory_space=pl.ANY)] * 9,
        out_specs=pl.BlockSpec(memory_space=pltpu.VMEM),
        scratch_shapes=[
            vmem((cell_count, 8, coefs), F32),
            vmem(upward_ops.shape, F32),
            vmem(transfer_ops.shape, F32),
            vmem(downward_ops.shape, F32),
            vmem(send_cells.shape[1:], jnp.int32),
            vmem(send_count.shape, jnp.int32),
            vmem(list_source.shape[1:], jnp.int32),
            vmem(list_target.shape[1:], jnp.int32),
            vmem(list_count.shape, jnp.int32),
            *weights(8),
            *weights(ops),
            *weights(8),
            vmem((ops * cell_count, rows), BF16),
            vmem((n_gz, slots, coefs), F32),
            vmem((n_gz, slots, coefs), F32),
            vmem((1, coefs), F32),
            vmem((devices, 1, coefs), F32),
            vmem((ops, cell_count + 16, coefs), BF16),
            vmem((ops, cell_count + 16, coefs), BF16),
            pltpu.SemaphoreType.DMA((9,)),
            pltpu.SemaphoreType.DMA((n_gz,)),
            pltpu.SemaphoreType.DMA((n_gz,)),
            pltpu.SemaphoreType.DMA,
            pltpu.SemaphoreType.DMA,
        ],
        compiler_params=pltpu.CompilerParams(
            collective_id=0, has_side_effects=True, vmem_limit_bytes=48 << 20
        ),
        cost_estimate=pl.CostEstimate(
            flops=6 * 2 * 32 * cell_count * coefs * coefs,
            bytes_accessed=8_000_000,
            transcendentals=0,
        ),
    )(leaf_multipoles.reshape(cell_count, 8, coefs), upward_ops, transfer_ops, downward_ops, *lists)
    return out.reshape(leaves, coefs)


def solution(mesh):
    sizes = tuple(mesh.shape[name] for name in ("gx", "gy", "gz"))
    split_all = ("gx", "gy", "gz")
    return jax.shard_map(
        functools.partial(local, sizes),
        mesh=mesh,
        in_specs=(
            P(split_all, None),
            P(),
            P(),
            P(),
            P(split_all, None, None),
            P(split_all, None),
            P(split_all, None, None),
            P(split_all, None, None),
            P(split_all, None),
        ),
        out_specs=P(split_all, None),
        check_vma=False,
    )
```

time: 136 us -> 23.2 us (0.17)
  blocking collectives: 41 us -> 0 us
  other arithmetic: 35.8 us -> 0 us
  matrix products: 31 us -> 0 us
  Pallas kernels: 0 us -> 19 us
  local copies, waits for them, and re-layouts: 19.8 us -> 3.95 us
  starting transfers between devices: 6.32 us -> 0 us
    unnamed x1 -> x0, blocking collectives: 41 us -> none
    dot_general x21 -> x0, matrix products: 29.9 us -> none  [the longest x16 22.6 us: one_operator(): jnp.dot(table[source], operator, precision=highest) * weights[:, None]]
    scatter-add x16 -> x0, other arithmetic: 21.7 us -> none  [one_operator(): return (total.at[target].add(product), None)]
    pallas_call x0 -> x1, Pallas kernels: none -> 19 us  [local(): pl.pallas_call(functools.partial(kernel, sizes), out_shape=jax.ShapeDtype...]
    gather x17 -> x0, local copies, waits for them, and re-layouts: 12.8 us -> none  [the longest x16 12.1 us: one_operator(): table[source]]
    select_n x18 -> x0, other arithmetic: 12.4 us -> none  [the longest x16 11.6 us: one_operator(): return (total.at[target].add(product), None)]
    all_to_all x1 -> x0, starting transfers between devices: 6.32 us -> none  [local(): lax.all_to_all(outgoing, 'gz', split_axis=0, concat_axis=0, tiled=True)]
    mul x32 -> x0, local copies, waits for them, and re-layouts: 1.79 us -> none  [one_operator(): jnp.dot(table[source], operator, precision=highest) * weights[:, None]]
  transfers between devices with their start and end apart: 1 -> 0, of which waited for: 0 -> 0; matrix products, arithmetic and copies ran while one was open for 5% -> 0% of each run, Pallas kernels for 0% -> 0%
where the time goes in v1:
time: 23.2 us; the launch traced here: 23 us
  Pallas kernels  19 us (82%)
  local copies, waits for them, and re-layouts  3.95 us (17%)
    pallas_call x1, Pallas kernels, local(): pl.pallas_call(functools.partial(kernel, sizes), out_shape=jax.ShapeDtype...  19 us
    unnamed x15, local copies, waits for them, and re-layouts  2.82 us
    reshape x1, local copies, waits for them, and re-layouts, local(): return out.reshape(leaves, coefs)  1.14 us

profile of v1, /device:TPU:0, one launch (start us, length us, event | category | flops | bytes accessed | tf_op | source)
XLA Modules:
  0.0 23.0 jit_solution(15435781382972380457)
XLA Ops:
  0.0 0.0 copy-start.6
  0.0 0.0 copy-start.3
  0.0 0.0 copy-start.2
  0.0 0.0 copy-start.5
  0.0 0.0 copy-start.4
  0.0 0.0 copy-start
  0.0 1.5 %copy.10 = f32[1024,152]{1,0:T(8,128)S(1)} copy(f32[1024,152]{0,1:T(8,128)} %param.9) | data formatting | bytes 1245184 | tf_op args[0]
  1.5 0.0 copy-done.6
  1.5 0.0 copy-done.3
  1.6 0.0 copy-done.2
  1.6 0.0 copy-done.5
  1.6 0.0 copy-done.4
  1.6 0.0 copy-done
  1.6 0.0 copy-start.1
  1.6 1.3 %copy-done.1 = f32[8,152,152]{2,1,0:T(8,128)S(1)} copy-done((f32[8,152,152]{2,1,0:T(8,128)S(1)}, f32[8,152,152]{2,1,0:T(8,128)}, u32[]{:S(2)}) %copy-start.1) | copy-done | bytes 739352
  2.9 19.0 %shard_map.91 = f32[128,8,152]{2,1,0:T(8,128)S(1)} custom-call(f32[128,8,152]{2,1,0:T(8,128)S(1)} %bitcast.3, f32[8,152,152]{2,1,0:T(8,128)S(1)} %copy-done, f32[16,152,152]{2,1,0:T(8,128)} %transfer_hbm.1, f32[8,152,152]{2,1,0:T(8,128)S(1)} %copy-done.1, s32[1,4,32]{2,1,0:T(4,128)S(1)} %copy-done.4, s32[1,4]{1,0:T(1,128)S(1)} %copy-done.5, ...), custom_call_target="tpu_custom_call" | custom-call | flops 1135607808 | bytes 8000000 | tf_op jit(solution)/shard_map/pallas_call | solution.py:229
  21.9 1.1 %copy.11 = f32[1024,152]{0,1:T(8,128)} copy(f32[1024,152]{1,0:T(8,128)S(1)} %bitcast.2) | data formatting | bytes 1245184 | tf_op jit(solution)/shard_map/reshape | solution.py:269
Async XLA Ops:
  0.0 1.5 %copy-start.6 = (s32[1,16]{1,0:T(1,128)S(1)}, s32[1,16]{1,0:T(1,128)}, u32[]{:S(2)}) copy-start(s32[1,16]{1,0:T(1,128)} %counts_hbm.1) | copy-start | bytes 196
  0.0 1.5 %copy-start.3 = (s32[1,16,128]{2,1,0:T(8,128)S(1)}, s32[1,16,128]{2,1,0:T(8,128)}, u32[]{:S(2)}) copy-start(s32[1,16,128]{2,1,0:T(8,128)} %target_hbm.1) | copy-start | bytes 24580
  0.0 1.6 %copy-start.2 = (s32[1,16,128]{2,1,0:T(8,128)S(1)}, s32[1,16,128]{2,1,0:T(8,128)}, u32[]{:S(2)}) copy-start(s32[1,16,128]{2,1,0:T(8,128)} %source_hbm.1) | copy-start | bytes 24580
  0.0 1.6 %copy-start.5 = (s32[1,4]{1,0:T(1,128)S(1)}, s32[1,4]{1,0:T(1,128)}, u32[]{:S(2)}) copy-start(s32[1,4]{1,0:T(1,128)} %sends_hbm.1) | copy-start | bytes 52
  0.0 1.6 %copy-start.4 = (s32[1,4,32]{2,1,0:T(4,128)S(1)}, s32[1,4,32]{2,1,0:T(4,128)}, u32[]{:S(2)}) copy-start(s32[1,4,32]{2,1,0:T(4,128)} %cells_hbm.1) | copy-start | bytes 1540
  0.0 1.6 %copy-start = (f32[8,152,152]{2,1,0:T(8,128)S(1)}, f32[8,152,152]{2,1,0:T(8,128)}, u32[]{:S(2)}) copy-start(f32[8,152,152]{2,1,0:T(8,128)} %up_hbm.1) | copy-start | bytes 2217988
  1.6 1.3 %copy-start.1 = (f32[8,152,152]{2,1,0:T(8,128)S(1)}, f32[8,152,152]{2,1,0:T(8,128)}, u32[]{:S(2)}) copy-start(f32[8,152,152]{2,1,0:T(8,128)} %down_hbm.1) | copy-start | bytes 2217988

commit v2 on v1

--- a/solution.py
+++ b/solution.py
@@ -47,13 +47,13 @@
     out_ref,
     leaf, up, transfer, down,
     cells, sends, source, target, counts,
-    up_high, up_low, transfer_high, transfer_low, down_high, down_low,
+    leaf_high, leaf_low, transfer_high, transfer_low, down_high, down_low,
     choose, outgoing, received, top_row, tops, picked_high, picked_low,
     load_sem, send_sem, recv_sem, top_send_sem, top_recv_sem,
 ):
     n_gx, n_gy, n_gz = sizes
     devices = n_gx * n_gy * n_gz
-    cell_count, _, coefs = leaf.shape
+    coefs, cell_count = leaf.shape[0], leaf.shape[1] // 8
     ops = transfer.shape[0]
     slots = cells.shape[1]
     rows = cell_count + n_gz * slots
@@ -77,13 +77,13 @@
         pltpu.make_async_copy(src, dst, load_sem.at[i])
         for i, (src, dst) in enumerate(
             [
+                (leaf_hbm, leaf),
+                (up_hbm, up),
+                (cells_hbm.at[0], cells),
+                (sends_hbm, sends),
                 (source_hbm.at[0], source),
                 (target_hbm.at[0], target),
                 (counts_hbm, counts),
-                (cells_hbm.at[0], cells),
-                (sends_hbm, sends),
-                (leaf_hbm, leaf),
-                (up_hbm, up),
                 (transfer_hbm, transfer),
                 (down_hbm, down),
             ]
@@ -99,17 +99,8 @@
         lambda x: pl.semaphore_signal(barrier, inc=1, device_id=peer(x), device_id_type=MESH),
     )
 
-    for load in loads[:5]:
-        load.wait()
-    lane = lax.broadcasted_iota(jnp.int32, (1, target.shape[1]), 1)
-    for k in range(ops):
-        used = jnp.where(lane < counts[0:1, k : k + 1], target[k : k + 1, :], -1)
-        choose[pl.ds(k * cell_count, cell_count), :] = lax.dot_general(
-            equal(used, cell_count),
-            equal(source[k : k + 1, :], rows),
-            NT,
-            preferred_element_type=F32,
-        ).astype(BF16)
+    loads[2].wait()
+    loads[3].wait()
     lane = lax.broadcasted_iota(jnp.int32, (1, slots), 1)
     wanted = jnp.concatenate(
         [
@@ -120,12 +111,19 @@
     )
     pick = equal(wanted, cell_count)
 
-    loads[5].wait()
-    loads[6].wait()
+    loads[0].wait()
+    wide = lax.broadcasted_iota(jnp.int32, (128, 128), 1)
+    tall = lax.broadcasted_iota(jnp.int32, (128, 128), 0)
+    group = jnp.where(wide == tall % 16 * 8 + tall // 16, 1.0, 0.0).astype(BF16)
+    for j in range(cell_count // 16):
+        for part, held in zip(split(leaf[:, 128 * j : 128 * j + 128]), (leaf_high, leaf_low)):
+            turned = lax.dot_general(group, part, NT, preferred_element_type=F32).astype(BF16)
+            for k in range(8):
+                held[k, 16 * j : 16 * j + 16, :] = turned[16 * k : 16 * k + 16]
+    loads[1].wait()
     cell = jnp.zeros((cell_count, coefs), F32)
     for k in range(8):
-        up_high[k], up_low[k] = split(up[k])
-        cell = cell + dot3(split(leaf[:, k, :]), (up_high[k], up_low[k]))
+        cell = cell + dot3((leaf_high[k], leaf_low[k]), split(up[k]))
     cell_high, cell_low = split(cell)
     out_rows = lax.dot_general(pick, cell_high, TN, preferred_element_type=F32) + lax.dot_general(
         pick, cell_low, TN, preferred_element_type=F32
@@ -148,11 +146,10 @@
     for copy in cell_copies:
         copy.start()
 
-    octants = split(cell.reshape(cell_count // 8, 8, coefs).sum(0))
-    top = jnp.zeros((8, coefs), F32)
-    eight = lax.broadcasted_iota(jnp.int32, (8, coefs), 0)
+    octants = cell.reshape(cell_count // 8, 8, coefs).sum(0).T
+    top = jnp.zeros((coefs, coefs), F32)
     for k in range(8):
-        top = top + jnp.where(eight == k, dot3(octants, (up_high[k], up_low[k])), 0.0)
+        top = top + octants[:, k : k + 1] * up[k]
     top_row[...] = (8.0 / cell_count) ** 0.5 * top.sum(0, keepdims=True)
 
     def send_top(x):
@@ -167,6 +164,18 @@
 
     each(n_gz, devices, send_top)
 
+    for load in loads[4:7]:
+        load.wait()
+    lane = lax.broadcasted_iota(jnp.int32, (1, target.shape[1]), 1)
+    for k in range(ops):
+        used = jnp.where(lane < counts[0:1, k : k + 1], target[k : k + 1, :], -1)
+        choose[pl.ds(k * cell_count, cell_count), :] = lax.dot_general(
+            equal(used, cell_count),
+            equal(source[k : k + 1, :], rows),
+            NT,
+            preferred_element_type=F32,
+        ).astype(BF16)
+
     loads[7].wait()
     for k in range(ops):
         transfer_high[k], transfer_low[k] = split(transfer[k])
@@ -185,28 +194,31 @@
         picked_high[k, 0:cell_count, :] = dot(chosen, table_high).astype(BF16)
         picked_low[k, 0:cell_count, :] = dot(chosen, table_low).astype(BF16)
 
-    far = tops.at[pl.ds(n_gz, devices - n_gz)]
-    pltpu.make_async_copy(far, far, top_recv_sem).wait()
-    for k in range(ops):
-        extra = jnp.zeros((1, coefs), F32)
-        for x in range(k, devices, ops):
-            if x >= n_gz:
-                extra = extra + tops[x]
-        picked_high[k, cell_count : cell_count + 16, :], picked_low[
-            k, cell_count : cell_count + 16, :
-        ] = split(jnp.broadcast_to(extra, (16, coefs)))
-    total = jnp.zeros((cell_count + 16, coefs), F32)
+    total = jnp.zeros((cell_count, coefs), F32)
     for k in range(ops):
         total = total + dot3(
             (picked_high[k], picked_low[k]), (transfer_high[k], transfer_low[k])
         )
-    coarse = split((32.0 / devices) ** 0.5 * total[cell_count:])
-    coarse_down = jnp.zeros((8, coefs), F32)
-    for k in range(8):
-        coarse_down = coarse_down + jnp.where(
-            eight == k, dot3(coarse, (down_high[k], down_low[k]))[0:8], 0.0
-        )
-    near = total[0:cell_count].reshape(cell_count // 8, 8, coefs)
+
+    far = tops.at[pl.ds(n_gz, devices - n_gz)]
+    pltpu.make_async_copy(far, far, top_recv_sem).wait()
+    far_rows = []
+    for k in range(ops):
+        row = jnp.zeros((1, coefs), F32)
+        for x in range(k, devices, ops):
+            if x >= n_gz:
+                row = row + tops[x]
+        far_rows.append(row)
+    far_columns = jnp.concatenate(far_rows, axis=0).T
+    coarse = jnp.zeros((coefs, coefs), F32)
+    for k in range(ops):
+        coarse = coarse + far_columns[:, k : k + 1] * transfer[k]
+    coarse = (32.0 / devices) ** 0.5 * coarse.sum(0, keepdims=True)
+    column = jnp.broadcast_to(coarse, (8, coefs)).T[:, 0:1]
+    coarse_down = jnp.concatenate(
+        [(column * down[k]).sum(0, keepdims=True) for k in range(8)], axis=0
+    )
+    near = total.reshape(cell_count // 8, 8, coefs)
     local_cells = split((near + coarse_down[None]).reshape(cell_count, coefs))
     for k in range(8):
         out_ref[:, k, :] = dot3(local_cells, (down_high[k], down_low[k]))
@@ -232,7 +244,7 @@
         in_specs=[pl.BlockSpec(memory_space=pl.ANY)] * 9,
         out_specs=pl.BlockSpec(memory_space=pltpu.VMEM),
         scratch_shapes=[
-            vmem((cell_count, 8, coefs), F32),
+            vmem((coefs, leaves), F32),
             vmem(upward_ops.shape, F32),
             vmem(transfer_ops.shape, F32),
             vmem(downward_ops.shape, F32),
@@ -241,7 +253,7 @@
             vmem(list_source.shape[1:], jnp.int32),
             vmem(list_target.shape[1:], jnp.int32),
             vmem(list_count.shape, jnp.int32),
-            *weights(8),
+            *[vmem((8, cell_count, coefs), BF16)] * 2,
             *weights(ops),
             *weights(8),
             vmem((ops * cell_count, rows), BF16),
@@ -249,8 +261,7 @@
             vmem((n_gz, slots, coefs), F32),
             vmem((1, coefs), F32),
             vmem((devices, 1, coefs), F32),
-            vmem((ops, cell_count + 16, coefs), BF16),
-            vmem((ops, cell_count + 16, coefs), BF16),
+            *[vmem((ops, cell_count, coefs), BF16)] * 2,
             pltpu.SemaphoreType.DMA((9,)),
             pltpu.SemaphoreType.DMA((n_gz,)),
             pltpu.SemaphoreType.DMA((n_gz,)),
@@ -258,14 +269,14 @@
             pltpu.SemaphoreType.DMA,
         ],
         compiler_params=pltpu.CompilerParams(
-            collective_id=0, has_side_effects=True, vmem_limit_bytes=48 << 20
+            collective_id=0, has_side_effects=True, vmem_limit_bytes=63 << 20
         ),
         cost_estimate=pl.CostEstimate(
             flops=6 * 2 * 32 * cell_count * coefs * coefs,
             bytes_accessed=8_000_000,
             transcendentals=0,
         ),
-    )(leaf_multipoles.reshape(cell_count, 8, coefs), upward_ops, transfer_ops, downward_ops, *lists)
+    )(leaf_multipoles.T, upward_ops, transfer_ops, downward_ops, *lists)
     return out.reshape(leaves, coefs)
 
 

time: 23.2 us -> 19.3 us (0.83)
  Pallas kernels: 19 us -> 16.8 us
  local copies, waits for them, and re-layouts: 3.95 us -> 2.36 us
    unnamed x15 -> x0, local copies, waits for them, and re-layouts: 2.82 us -> none
    pallas_call x1, Pallas kernels: 19 us -> 16.8 us  [local(): pl.pallas_call(functools.partial(kernel, sizes), out_shape=jax.ShapeDtype...]
    reshape x1, local copies, waits for them, and re-layouts: 1.14 us -> 2.36 us  [local(): return out.reshape(leaves, coefs)]
where the time goes in v2:
time: 19.3 us; the launch traced here: 19.1 us
  Pallas kernels  16.8 us (87%)
  local copies, waits for them, and re-layouts  2.36 us (12%)
    pallas_call x1, Pallas kernels, local(): pl.pallas_call(functools.partial(kernel, sizes), out_shape=jax.ShapeDtype...  16.8 us
    reshape x1, local copies, waits for them, and re-layouts, local(): return out.reshape(leaves, coefs)  2.36 us

profile of v2, /device:TPU:0, one launch (start us, length us, event | category | flops | bytes accessed | tf_op | source)
XLA Modules:
  0.0 19.1 jit_solution(12743274576510276287)
XLA Ops:
  0.0 16.8 %shard_map.91 = f32[128,8,152]{2,1,0:T(8,128)} custom-call(f32[152,1024]{1,0:T(8,128)} %bitcast.3, f32[8,152,152]{2,1,0:T(8,128)} %up_hbm.1, f32[16,152,152]{2,1,0:T(8,128)} %transfer_hbm.1, f32[8,152,152]{2,1,0:T(8,128)} %down_hbm.1, s32[1,4,32]{2,1,0:T(4,128)} %cells_hbm.1, s32[1,4]{1,0:T(1,128)} %sends_hbm.1, s32[1,16,128]{2,1,0:T(8,128)} %source_hbm.1, ...), custom_call_target="tpu_custom_call" | custom-call | flops 1135607808 | bytes 8000000 | tf_op jit(solution)/shard_map/pallas_call | solution.py:241
  16.8 2.4 %copy.10 = f32[1024,152]{0,1:T(8,128)} copy(f32[1024,152]{1,0:T(8,128)} %bitcast.2) | data formatting | bytes 1245184 | tf_op jit(solution)/shard_map/reshape | solution.py:280

commit v3 on v2

--- a/solution.py
+++ b/solution.py
@@ -23,8 +23,10 @@
     return jnp.dot(a, b, preferred_element_type=F32)
 
 
-def dot3(a, b):
-    return dot(a[0], b[0]) + dot(a[0], b[1]) + dot(a[1], b[0])
+def dot3(both, high, low):
+    half = both.shape[0] // 2
+    wide = dot(both, high)
+    return wide[:half] + wide[half:] + dot(both[:half], low)
 
 
 def xor(a, b, size):
@@ -47,8 +49,8 @@
     out_ref,
     leaf, up, transfer, down,
     cells, sends, source, target, counts,
-    leaf_high, leaf_low, transfer_high, transfer_low, down_high, down_low,
-    choose, outgoing, received, top_row, tops, picked_high, picked_low,
+    leaf_both, transfer_high, transfer_low, down_high, down_low,
+    choose, outgoing, received, top_row, tops, picked, staged,
     load_sem, send_sem, recv_sem, top_send_sem, top_recv_sem,
 ):
     n_gx, n_gy, n_gz = sizes
@@ -116,14 +118,14 @@
     tall = lax.broadcasted_iota(jnp.int32, (128, 128), 0)
     group = jnp.where(wide == tall % 16 * 8 + tall // 16, 1.0, 0.0).astype(BF16)
     for j in range(cell_count // 16):
-        for part, held in zip(split(leaf[:, 128 * j : 128 * j + 128]), (leaf_high, leaf_low)):
+        for part, first in zip(split(leaf[:, 128 * j : 128 * j + 128]), (0, cell_count)):
             turned = lax.dot_general(group, part, NT, preferred_element_type=F32).astype(BF16)
             for k in range(8):
-                held[k, 16 * j : 16 * j + 16, :] = turned[16 * k : 16 * k + 16]
+                leaf_both[
+                    first + 16 * j : first + 16 * j + 16, coefs * k : coefs * k + coefs
+                ] = turned[16 * k : 16 * k + 16]
     loads[1].wait()
-    cell = jnp.zeros((cell_count, coefs), F32)
-    for k in range(8):
-        cell = cell + dot3((leaf_high[k], leaf_low[k]), split(up[k]))
+    cell = dot3(leaf_both[...], *split(up[...].reshape(8 * coefs, coefs)))
     cell_high, cell_low = split(cell)
     out_rows = lax.dot_general(pick, cell_high, TN, preferred_element_type=F32) + lax.dot_general(
         pick, cell_low, TN, preferred_element_type=F32
@@ -177,8 +179,7 @@
         ).astype(BF16)
 
     loads[7].wait()
-    for k in range(ops):
-        transfer_high[k], transfer_low[k] = split(transfer[k])
+    transfer_high[...], transfer_low[...] = split(transfer[...].reshape(ops * coefs, coefs))
     loads[8].wait()
     for k in range(8):
         down_high[k], down_low[k] = split(down[k])
@@ -189,16 +190,16 @@
     got_high, got_low = split(received[...].reshape(n_gz * slots, coefs))
     table_high = jnp.concatenate([cell_high, got_high], axis=0)
     table_low = jnp.concatenate([cell_low, got_low], axis=0)
-    for k in range(ops):
-        chosen = choose[pl.ds(k * cell_count, cell_count), :]
-        picked_high[k, 0:cell_count, :] = dot(chosen, table_high).astype(BF16)
-        picked_low[k, 0:cell_count, :] = dot(chosen, table_low).astype(BF16)
-
-    total = jnp.zeros((cell_count, coefs), F32)
-    for k in range(ops):
-        total = total + dot3(
-            (picked_high[k], picked_low[k]), (transfer_high[k], transfer_low[k])
-        )
+    step = 4 * cell_count
+    for part, first in ((table_high, 0), (table_low, cell_count)):
+        for start in range(0, ops * cell_count, step):
+            rows_picked = dot(choose[start : start + step, :], part).astype(BF16)
+            for k in range(4):
+                lane = coefs * (start // cell_count + k)
+                picked[first : first + cell_count, lane : lane + coefs] = rows_picked[
+                    cell_count * k : cell_count * k + cell_count
+                ]
+    total = dot3(picked[...], transfer_high[...], transfer_low[...])
 
     far = tops.at[pl.ds(n_gz, devices - n_gz)]
     pltpu.make_async_copy(far, far, top_recv_sem).wait()
@@ -219,9 +220,16 @@
         [(column * down[k]).sum(0, keepdims=True) for k in range(8)], axis=0
     )
     near = total.reshape(cell_count // 8, 8, coefs)
-    local_cells = split((near + coarse_down[None]).reshape(cell_count, coefs))
+    local_cells = (near + coarse_down[None]).reshape(cell_count, coefs)
+    both = jnp.concatenate(split(local_cells), axis=0)
     for k in range(8):
-        out_ref[:, k, :] = dot3(local_cells, (down_high[k], down_low[k]))
+        staged[:, k, :] = dot3(both, down_high[k], down_low[k])
+    same = equal(lax.broadcasted_iota(jnp.int32, (1, coefs), 1), coefs)
+    for j in range(cell_count // 32):
+        high, low = split(staged[32 * j : 32 * j + 32].reshape(256, coefs))
+        out_ref[:, 256 * j : 256 * j + 256] = lax.dot_general(
+            same, high, NT, preferred_element_type=F32
+        ) + lax.dot_general(same, low, NT, preferred_element_type=F32)
 
     for copy in cell_copies:
         copy.wait_send()
@@ -240,8 +248,8 @@
     weights = lambda n: [vmem((n, coefs, coefs), BF16)] * 2
     out = pl.pallas_call(
         functools.partial(kernel, sizes),
-        out_shape=jax.ShapeDtypeStruct((cell_count, 8, coefs), F32),
-        in_specs=[pl.BlockSpec(memory_space=pl.ANY)] * 9,
+        out_shape=jax.ShapeDtypeStruct((coefs, leaves), F32),
+        in_specs=[pl.BlockSpec(memory_space=pltpu.HBM)] * 9,
         out_specs=pl.BlockSpec(memory_space=pltpu.VMEM),
         scratch_shapes=[
             vmem((coefs, leaves), F32),
@@ -253,15 +261,16 @@
             vmem(list_source.shape[1:], jnp.int32),
             vmem(list_target.shape[1:], jnp.int32),
             vmem(list_count.shape, jnp.int32),
-            *[vmem((8, cell_count, coefs), BF16)] * 2,
-            *weights(ops),
+            vmem((2 * cell_count, 8 * coefs), BF16),
+            *[vmem((ops * coefs, coefs), BF16)] * 2,
             *weights(8),
             vmem((ops * cell_count, rows), BF16),
             vmem((n_gz, slots, coefs), F32),
             vmem((n_gz, slots, coefs), F32),
             vmem((1, coefs), F32),
             vmem((devices, 1, coefs), F32),
-            *[vmem((ops, cell_count, coefs), BF16)] * 2,
+            vmem((2 * cell_count, ops * coefs), BF16),
+            vmem((cell_count, 8, coefs), F32),
             pltpu.SemaphoreType.DMA((9,)),
             pltpu.SemaphoreType.DMA((n_gz,)),
             pltpu.SemaphoreType.DMA((n_gz,)),
@@ -269,7 +278,7 @@
             pltpu.SemaphoreType.DMA,
         ],
         compiler_params=pltpu.CompilerParams(
-            collective_id=0, has_side_effects=True, vmem_limit_bytes=63 << 20
+            collective_id=0, has_side_effects=True, vmem_limit_bytes=53 << 20
         ),
         cost_estimate=pl.CostEstimate(
             flops=6 * 2 * 32 * cell_count * coefs * coefs,
@@ -277,7 +286,7 @@
             transcendentals=0,
         ),
     )(leaf_multipoles.T, upward_ops, transfer_ops, downward_ops, *lists)
-    return out.reshape(leaves, coefs)
+    return out.T
 
 
 def solution(mesh):

time: 19.3 us -> 20.4 us (1.057)
  local copies, waits for them, and re-layouts: 2.36 us -> 4.21 us
  Pallas kernels: 16.8 us -> 15.8 us
    unnamed x0 -> x11, local copies, waits for them, and re-layouts: none -> 4.21 us
    reshape x1 -> x0, local copies, waits for them, and re-layouts: 2.36 us -> none  [local(): return out.reshape(leaves, coefs)]
    pallas_call x1, Pallas kernels: 16.8 us -> 15.8 us  [local(): pl.pallas_call(functools.partial(kernel, sizes), out_shape=jax.ShapeDtype...]
where the time goes in v3:
time: 20.4 us; the launch traced here: 20.1 us
  Pallas kernels  15.8 us (77%)
  local copies, waits for them, and re-layouts  4.21 us (21%)
    pallas_call x1, Pallas kernels, local(): pl.pallas_call(functools.partial(kernel, sizes), out_shape=jax.ShapeDtype...  15.8 us
    unnamed x11, local copies, waits for them, and re-layouts  4.21 us

profile of v3, /device:TPU:0, one launch (start us, length us, event | category | flops | bytes accessed | tf_op | source)
XLA Modules:
  0.0 20.1 jit_solution(8582365103947983039)
XLA Ops:
  0.0 0.0 copy-start
  0.0 0.7 %copy-done = s32[1,16,128]{2,1,0:T(8,128)S(1)} copy-done((s32[1,16,128]{2,1,0:T(8,128)S(1)}, s32[1,16,128]{2,1,0:T(8,128)}, u32[]{:S(2)}) %copy-start) | copy-done | bytes 8216
  0.7 0.0 copy-start.1
  0.7 0.7 %copy-done.1 = s32[1,16,128]{2,1,0:T(8,128)S(1)} copy-done((s32[1,16,128]{2,1,0:T(8,128)S(1)}, s32[1,16,128]{2,1,0:T(8,128)}, u32[]{:S(2)}) %copy-start.1) | copy-done | bytes 8216
  1.4 0.0 copy-start.2
  1.4 0.7 %copy-done.2 = s32[1,4,32]{2,1,0:T(4,128)S(1)} copy-done((s32[1,4,32]{2,1,0:T(4,128)S(1)}, s32[1,4,32]{2,1,0:T(4,128)}, u32[]{:S(2)}) %copy-start.2) | copy-done | bytes 536
  2.1 0.0 copy-start.3
  2.1 0.7 %copy-done.3 = s32[1,4]{1,0:T(1,128)S(1)} copy-done((s32[1,4]{1,0:T(1,128)S(1)}, s32[1,4]{1,0:T(1,128)}, u32[]{:S(2)}) %copy-start.3) | copy-done | bytes 40
  2.7 0.0 copy-start.4
  2.7 0.7 %copy-done.4 = s32[1,16]{1,0:T(1,128)S(1)} copy-done((s32[1,16]{1,0:T(1,128)S(1)}, s32[1,16]{1,0:T(1,128)}, u32[]{:S(2)}) %copy-start.4) | copy-done | bytes 88
  3.4 15.8 %shard_map.91 = f32[152,1024]{1,0:T(8,128)S(1)} custom-call(f32[152,1024]{1,0:T(8,128)} %bitcast.3, f32[8,152,152]{2,1,0:T(8,128)} %up_hbm.1, f32[16,152,152]{2,1,0:T(8,128)} %transfer_hbm.1, f32[8,152,152]{2,1,0:T(8,128)} %down_hbm.1, s32[1,4,32]{2,1,0:T(4,128)S(1)} %copy-done.2, s32[1,4]{1,0:T(1,128)S(1)} %copy-done.3, s32[1,16,128]{2,1,0:T(8,128)S(1)} %copy-done, ...), custom_call_target="tpu_custom_call" | custom-call | flops 1135607808 | bytes 8000000 | tf_op jit(solution)/shard_map/pallas_call | solution.py:249
  19.2 0.8 %copy.11 = f32[1024,152]{0,1:T(8,128)} copy(f32[1024,152]{0,1:T(8,128)S(1)} %bitcast.2) | data formatting | bytes 1245184
Async XLA Ops:
  0.0 0.7 %copy-start = (s32[1,16,128]{2,1,0:T(8,128)S(1)}, s32[1,16,128]{2,1,0:T(8,128)}, u32[]{:S(2)}) copy-start(s32[1,16,128]{2,1,0:T(8,128)} %source_hbm.1) | copy-start | bytes 24580
  0.7 0.7 %copy-start.1 = (s32[1,16,128]{2,1,0:T(8,128)S(1)}, s32[1,16,128]{2,1,0:T(8,128)}, u32[]{:S(2)}) copy-start(s32[1,16,128]{2,1,0:T(8,128)} %target_hbm.1) | copy-start | bytes 24580
  1.4 0.7 %copy-start.2 = (s32[1,4,32]{2,1,0:T(4,128)S(1)}, s32[1,4,32]{2,1,0:T(4,128)}, u32[]{:S(2)}) copy-start(s32[1,4,32]{2,1,0:T(4,128)} %cells_hbm.1) | copy-start | bytes 1540
  2.1 0.7 %copy-start.3 = (s32[1,4]{1,0:T(1,128)S(1)}, s32[1,4]{1,0:T(1,128)}, u32[]{:S(2)}) copy-start(s32[1,4]{1,0:T(1,128)} %sends_hbm.1) | copy-start | bytes 52
  2.7 0.7 %copy-start.4 = (s32[1,16]{1,0:T(1,128)S(1)}, s32[1,16]{1,0:T(1,128)}, u32[]{:S(2)}) copy-start(s32[1,16]{1,0:T(1,128)} %counts_hbm.1) | copy-start | bytes 196

commit v4 on v3

--- a/solution.py
+++ b/solution.py
@@ -246,6 +246,7 @@
     rows = cell_count + n_gz * slots
     vmem = pltpu.VMEM
     weights = lambda n: [vmem((n, coefs, coefs), BF16)] * 2
+    operands = (leaf_multipoles.T, upward_ops, transfer_ops, downward_ops, *lists)
     out = pl.pallas_call(
         functools.partial(kernel, sizes),
         out_shape=jax.ShapeDtypeStruct((coefs, leaves), F32),
@@ -278,14 +279,14 @@
             pltpu.SemaphoreType.DMA,
         ],
         compiler_params=pltpu.CompilerParams(
-            collective_id=0, has_side_effects=True, vmem_limit_bytes=53 << 20
+            collective_id=0, has_side_effects=True, vmem_limit_bytes=48 << 20
         ),
         cost_estimate=pl.CostEstimate(
             flops=6 * 2 * 32 * cell_count * coefs * coefs,
             bytes_accessed=8_000_000,
             transcendentals=0,
         ),
-    )(leaf_multipoles.T, upward_ops, transfer_ops, downward_ops, *lists)
+    )(*(pltpu.with_memory_space_constraint(x, pltpu.HBM) for x in operands))
     return out.T
 
 

time: 20.4 us -> 16.8 us (0.82)
  local copies, waits for them, and re-layouts: 4.21 us -> 0.83 us
    unnamed x11 -> x1, local copies, waits for them, and re-layouts: 4.21 us -> 0.83 us
where the time goes in v4:
time: 16.8 us; the launch traced here: 16.6 us
  Pallas kernels  15.8 us (94%)
  local copies, waits for them, and re-layouts  0.83 us (5%)
    pallas_call x1, Pallas kernels, local(): pl.pallas_call(functools.partial(kernel, sizes), out_shape=jax.ShapeDtype...  15.8 us
    unnamed x1, local copies, waits for them, and re-layouts  0.83 us

profile of v4, /device:TPU:0, one launch (start us, length us, event | category | flops | bytes accessed | tf_op | source)
XLA Modules:
  0.0 16.6 jit_solution(11884746781783796446)
XLA Ops:
  0.0 15.8 %shard_map.91 = f32[152,1024]{1,0:T(8,128)S(1)} custom-call(f32[152,1024]{1,0:T(8,128)} %bitcast.3, f32[8,152,152]{2,1,0:T(8,128)} %up_hbm.1, f32[16,152,152]{2,1,0:T(8,128)} %transfer_hbm.1, f32[8,152,152]{2,1,0:T(8,128)} %down_hbm.1, s32[1,4,32]{2,1,0:T(4,128)} %cells_hbm.1, s32[1,4]{1,0:T(1,128)} %sends_hbm.1, s32[1,16,128]{2,1,0:T(8,128)} %source_hbm.1, ...), custom_call_target="tpu_custom_call" | custom-call | flops 1135607808 | bytes 8000000 | tf_op jit(solution)/shard_map/pallas_call | solution.py:250
  15.8 0.8 %copy.11 = f32[1024,152]{0,1:T(8,128)} copy(f32[1024,152]{0,1:T(8,128)S(1)} %bitcast.2) | data formatting | bytes 1245184

commit v5 on v4

--- a/solution.py
+++ b/solution.py
@@ -29,12 +29,21 @@
     return wide[:half] + wide[half:] + dot(both[:half], low)
 
 
-def xor(a, b, size):
-    total, bit = 0, 1
-    while bit < size:
-        total = total + ((a // bit + b // bit) % 2) * bit
-        bit *= 2
-    return total
+def flips(place, size):
+    bits = []
+    while 1 << len(bits) < size:
+        bit = 1 << len(bits)
+        bits.append(bit - 2 * bit * lax.rem(lax.div(place, bit), 2))
+    return bits
+
+
+def xor(place, bits, x):
+    for i, step in enumerate(bits):
+        if isinstance(x, int):
+            place = place + step if x >> i & 1 else place
+        else:
+            place = place + step * lax.rem(lax.div(x, 1 << i), 2)
+    return place
 
 
 def equal(row, length):
@@ -61,11 +70,17 @@
     rows = cell_count + n_gz * slots
     i_gx, i_gy, i_gz = lax.axis_index("gx"), lax.axis_index("gy"), lax.axis_index("gz")
 
+    places = [(i_gx, n_gx, n_gy * n_gz), (i_gy, n_gy, n_gz), (i_gz, n_gz, 1)]
+    axes = [(place, flips(place, size), size, below) for place, size, below in places]
+    known = [[xor(p, bits, v) for v in range(size)] for p, bits, size, _ in axes]
+
     def peer(x):
-        return (
-            xor(i_gx, x // (n_gz * n_gy), n_gx),
-            xor(i_gy, (x // n_gz) % n_gy, n_gy),
-            xor(i_gz, x % n_gz, n_gz),
+        if isinstance(x, int):
+            return tuple(
+                table[x // below % size] for table, (_, _, size, below) in zip(known, axes)
+            )
+        return tuple(
+            xor(p, bits, lax.rem(lax.div(x, below), size)) for p, bits, size, below in axes
         )
 
     def each(low, high, body):
@@ -91,7 +106,7 @@
             ]
         )
     ]
-    for load in loads:
+    for load in loads[:7]:
         load.start()
 
     barrier = pltpu.get_barrier_semaphore()
@@ -114,6 +129,9 @@
     pick = equal(wanted, cell_count)
 
     loads[0].wait()
+    loads[1].wait()
+    loads[7].start()
+    loads[8].start()
     wide = lax.broadcasted_iota(jnp.int32, (128, 128), 1)
     tall = lax.broadcasted_iota(jnp.int32, (128, 128), 0)
     group = jnp.where(wide == tall % 16 * 8 + tall // 16, 1.0, 0.0).astype(BF16)
@@ -124,13 +142,17 @@
                 leaf_both[
                     first + 16 * j : first + 16 * j + 16, coefs * k : coefs * k + coefs
                 ] = turned[16 * k : 16 * k + 16]
-    loads[1].wait()
     cell = dot3(leaf_both[...], *split(up[...].reshape(8 * coefs, coefs)))
     cell_high, cell_low = split(cell)
     out_rows = lax.dot_general(pick, cell_high, TN, preferred_element_type=F32) + lax.dot_general(
         pick, cell_low, TN, preferred_element_type=F32
     )
     outgoing[...] = out_rows.reshape(n_gz, slots, coefs)
+    octants = cell.reshape(cell_count // 8, 8, coefs).sum(0).T
+    top = jnp.zeros((coefs, coefs), F32)
+    for k in range(8):
+        top = top + octants[:, k : k + 1] * up[k]
+    top_row[...] = (8.0 / cell_count) ** 0.5 * top.sum(0, keepdims=True)
     pl.semaphore_wait(barrier, devices - 1)
 
     def cell_copy(x):
@@ -147,12 +169,6 @@
     cell_copies = [cell_copy(x) for x in range(1, n_gz)]
     for copy in cell_copies:
         copy.start()
-
-    octants = cell.reshape(cell_count // 8, 8, coefs).sum(0).T
-    top = jnp.zeros((coefs, coefs), F32)
-    for k in range(8):
-        top = top + octants[:, k : k + 1] * up[k]
-    top_row[...] = (8.0 / cell_count) ** 0.5 * top.sum(0, keepdims=True)
 
     def send_top(x):
         pltpu.make_async_remote_copy(

time: 16.8 us -> 16.8 us (level)
  no operation moved by 1% of the time
where the time goes in v5:
time: 16.8 us; the launch traced here: 16.7 us
  Pallas kernels  15.8 us (94%)
  local copies, waits for them, and re-layouts  0.83 us (5%)
    pallas_call x1, Pallas kernels, local(): pl.pallas_call(functools.partial(kernel, sizes), out_shape=jax.ShapeDtype...  15.8 us
    unnamed x1, local copies, waits for them, and re-layouts  0.83 us

profile of v5, /device:TPU:0, one launch (start us, length us, event | category | flops | bytes accessed | tf_op | source)
XLA Modules:
  0.0 16.7 jit_solution(1623934942447501045)
XLA Ops:
  0.0 15.8 %shard_map.91 = f32[152,1024]{1,0:T(8,128)S(1)} custom-call(f32[152,1024]{1,0:T(8,128)} %bitcast.3, f32[8,152,152]{2,1,0:T(8,128)} %up_hbm.1, f32[16,152,152]{2,1,0:T(8,128)} %transfer_hbm.1, f32[8,152,152]{2,1,0:T(8,128)} %down_hbm.1, s32[1,4,32]{2,1,0:T(4,128)} %cells_hbm.1, s32[1,4]{1,0:T(1,128)} %sends_hbm.1, s32[1,16,128]{2,1,0:T(8,128)} %source_hbm.1, ...), custom_call_target="tpu_custom_call" | custom-call | flops 1135607808 | bytes 8000000 | tf_op jit(solution)/shard_map/pallas_call | solution.py:266
  15.8 0.8 %copy.11 = f32[1024,152]{0,1:T(8,128)} copy(f32[1024,152]{0,1:T(8,128)S(1)} %bitcast.2) | data formatting | bytes 1245184

commit v6 on v5

--- a/solution.py
+++ b/solution.py
@@ -132,16 +132,10 @@
     loads[1].wait()
     loads[7].start()
     loads[8].start()
-    wide = lax.broadcasted_iota(jnp.int32, (128, 128), 1)
-    tall = lax.broadcasted_iota(jnp.int32, (128, 128), 0)
-    group = jnp.where(wide == tall % 16 * 8 + tall // 16, 1.0, 0.0).astype(BF16)
-    for j in range(cell_count // 16):
-        for part, first in zip(split(leaf[:, 128 * j : 128 * j + 128]), (0, cell_count)):
-            turned = lax.dot_general(group, part, NT, preferred_element_type=F32).astype(BF16)
-            for k in range(8):
-                leaf_both[
-                    first + 16 * j : first + 16 * j + 16, coefs * k : coefs * k + coefs
-                ] = turned[16 * k : 16 * k + 16]
+    staged[...] = leaf[...].T.reshape(cell_count, 8, coefs)
+    for k in range(8):
+        lanes = slice(coefs * k, coefs * k + coefs)
+        leaf_both[0:cell_count, lanes], leaf_both[cell_count:, lanes] = split(staged[:, k, :])
     cell = dot3(leaf_both[...], *split(up[...].reshape(8 * coefs, coefs)))
     cell_high, cell_low = split(cell)
     out_rows = lax.dot_general(pick, cell_high, TN, preferred_element_type=F32) + lax.dot_general(
@@ -240,12 +234,7 @@
     both = jnp.concatenate(split(local_cells), axis=0)
     for k in range(8):
         staged[:, k, :] = dot3(both, down_high[k], down_low[k])
-    same = equal(lax.broadcasted_iota(jnp.int32, (1, coefs), 1), coefs)
-    for j in range(cell_count // 32):
-        high, low = split(staged[32 * j : 32 * j + 32].reshape(256, coefs))
-        out_ref[:, 256 * j : 256 * j + 256] = lax.dot_general(
-            same, high, NT, preferred_element_type=F32
-        ) + lax.dot_general(same, low, NT, preferred_element_type=F32)
+    out_ref[...] = staged[...].reshape(8 * cell_count, coefs).T
 
     for copy in cell_copies:
         copy.wait_send()

time: 16.8 us -> 19.2 us (1.14)
  Pallas kernels: 15.8 us -> 18.3 us
    pallas_call x1, Pallas kernels: 15.8 us -> 18.3 us  [local(): pl.pallas_call(functools.partial(kernel, sizes), out_shape=jax.ShapeDtype...]
where the time goes in v6:
time: 19.2 us; the launch traced here: 19.1 us
  Pallas kernels  18.3 us (95%)
  local copies, waits for them, and re-layouts  0.83 us (4%)
    pallas_call x1, Pallas kernels, local(): pl.pallas_call(functools.partial(kernel, sizes), out_shape=jax.ShapeDtype...  18.3 us
    unnamed x1, local copies, waits for them, and re-layouts  0.83 us

profile of v6, /device:TPU:0, one launch (start us, length us, event | category | flops | bytes accessed | tf_op | source)
XLA Modules:
  0.0 19.1 jit_solution(9026612511558539492)
XLA Ops:
  0.0 18.3 %shard_map.91 = f32[152,1024]{1,0:T(8,128)S(1)} custom-call(f32[152,1024]{1,0:T(8,128)} %bitcast.3, f32[8,152,152]{2,1,0:T(8,128)} %up_hbm.1, f32[16,152,152]{2,1,0:T(8,128)} %transfer_hbm.1, f32[8,152,152]{2,1,0:T(8,128)} %down_hbm.1, s32[1,4,32]{2,1,0:T(4,128)} %cells_hbm.1, s32[1,4]{1,0:T(1,128)} %sends_hbm.1, s32[1,16,128]{2,1,0:T(8,128)} %source_hbm.1, ...), custom_call_target="tpu_custom_call" | custom-call | flops 1135607808 | bytes 8000000 | tf_op jit(solution)/shard_map/pallas_call | solution.py:255
  18.3 0.8 %copy.11 = f32[1024,152]{0,1:T(8,128)} copy(f32[1024,152]{0,1:T(8,128)S(1)} %bitcast.2) | data formatting | bytes 1245184

commit v7 on v5

--- a/solution.py
+++ b/solution.py
@@ -60,7 +60,7 @@
     cells, sends, source, target, counts,
     leaf_both, transfer_high, transfer_low, down_high, down_low,
     choose, outgoing, received, top_row, tops, picked, staged,
-    load_sem, send_sem, recv_sem, top_send_sem, top_recv_sem,
+    load_sem, up_sem, send_sem, recv_sem, top_send_sem, top_recv_sem,
 ):
     n_gx, n_gy, n_gz = sizes
     devices = n_gx * n_gy * n_gz
@@ -106,7 +106,10 @@
             ]
         )
     ]
-    for load in loads[:7]:
+    up_loads = [
+        pltpu.make_async_copy(up_hbm.at[k], up.at[k], up_sem.at[k]) for k in range(8)
+    ]
+    for load in [loads[0], *up_loads, *loads[2:7]]:
         load.start()
 
     barrier = pltpu.get_barrier_semaphore()
@@ -129,19 +132,20 @@
     pick = equal(wanted, cell_count)
 
     loads[0].wait()
-    loads[1].wait()
-    loads[7].start()
-    loads[8].start()
-    wide = lax.broadcasted_iota(jnp.int32, (128, 128), 1)
-    tall = lax.broadcasted_iota(jnp.int32, (128, 128), 0)
-    group = jnp.where(wide == tall % 16 * 8 + tall // 16, 1.0, 0.0).astype(BF16)
-    for j in range(cell_count // 16):
-        for part, first in zip(split(leaf[:, 128 * j : 128 * j + 128]), (0, cell_count)):
+    wide = lax.broadcasted_iota(jnp.int32, (256, 256), 1)
+    tall = lax.broadcasted_iota(jnp.int32, (256, 256), 0)
+    group = jnp.where(wide == tall % 32 * 8 + tall // 32, 1.0, 0.0).astype(BF16)
+    for j in range(cell_count // 32):
+        for part, first in zip(split(leaf[:, 256 * j : 256 * j + 256]), (0, cell_count)):
             turned = lax.dot_general(group, part, NT, preferred_element_type=F32).astype(BF16)
             for k in range(8):
                 leaf_both[
-                    first + 16 * j : first + 16 * j + 16, coefs * k : coefs * k + coefs
-                ] = turned[16 * k : 16 * k + 16]
+                    first + 32 * j : first + 32 * j + 32, coefs * k : coefs * k + coefs
+                ] = turned[32 * k : 32 * k + 32]
+    for load in up_loads:
+        load.wait()
+    loads[7].start()
+    loads[8].start()
     cell = dot3(leaf_both[...], *split(up[...].reshape(8 * coefs, coefs)))
     cell_high, cell_low = split(cell)
     out_rows = lax.dot_general(pick, cell_high, TN, preferred_element_type=F32) + lax.dot_general(
@@ -289,6 +293,7 @@
             vmem((2 * cell_count, ops * coefs), BF16),
             vmem((cell_count, 8, coefs), F32),
             pltpu.SemaphoreType.DMA((9,)),
+            pltpu.SemaphoreType.DMA((8,)),
             pltpu.SemaphoreType.DMA((n_gz,)),
             pltpu.SemaphoreType.DMA((n_gz,)),
             pltpu.SemaphoreType.DMA,

time: 16.8 us -> 16.8 us (level)
  no operation moved by 1% of the time
where the time goes in v7:
time: 16.8 us; the launch traced here: 16.7 us
  Pallas kernels  15.9 us (95%)
  local copies, waits for them, and re-layouts  0.83 us (5%)
    pallas_call x1, Pallas kernels, local(): pl.pallas_call(functools.partial(kernel, sizes), out_shape=jax.ShapeDtype...  15.9 us
    unnamed x1, local copies, waits for them, and re-layouts  0.83 us

profile of v7, /device:TPU:0, one launch (start us, length us, event | category | flops | bytes accessed | tf_op | source)
XLA Modules:
  0.0 16.7 jit_solution(16896563463167275767)
XLA Ops:
  0.0 15.9 %shard_map.91 = f32[152,1024]{1,0:T(8,128)S(1)} custom-call(f32[152,1024]{1,0:T(8,128)} %bitcast.3, f32[8,152,152]{2,1,0:T(8,128)} %up_hbm.1, f32[16,152,152]{2,1,0:T(8,128)} %transfer_hbm.1, f32[8,152,152]{2,1,0:T(8,128)} %down_hbm.1, s32[1,4,32]{2,1,0:T(4,128)} %cells_hbm.1, s32[1,4]{1,0:T(1,128)} %sends_hbm.1, s32[1,16,128]{2,1,0:T(8,128)} %source_hbm.1, ...), custom_call_target="tpu_custom_call" | custom-call | flops 1135607808 | bytes 8000000 | tf_op jit(solution)/shard_map/pallas_call | solution.py:270
  15.9 0.8 %copy.11 = f32[1024,152]{0,1:T(8,128)} copy(f32[1024,152]{0,1:T(8,128)S(1)} %bitcast.2) | data formatting | bytes 1245184
